TPU v7x, 1024 devices: a whole 4x8x16 slice. The times are simulated.
1024 devices in a mesh: fsdp: 32 (over y_hi, x, core), tp: 32 (over y_lo, z).
Axes of the slice: x: 4, y: 8 (y_hi: 4, y_lo: 2; y = y_hi * 2 + y_lo), z: 16, core: 2. Of those that a mesh axis runs over, the one named last changes fastest.
Arguments:
- tokens: bfloat16 [512, 12288], P('tp', 'fsdp'), may hold values from -6 to 6
- up_weight: bfloat16 [12288, 28672], P('fsdp', 'tp'), may hold values from -0.0546875 to 0.0546875
- down_weight: bfloat16 [28672, 12288], P('tp', 'fsdp'), may hold values from -0.03125 to 0.03125
- out_grad: bfloat16 [512, 12288], P('tp', 'fsdp'), may hold values from -6 to 6
Outputs:
- output: bfloat16 [512, 12288], P('tp', 'fsdp')
- in_grad: bfloat16 [512, 12288], P('tp', 'fsdp')
- up_grad: bfloat16 [12288, 28672], P('fsdp', 'tp')
- down_grad: bfloat16 [28672, 12288], P('tp', 'fsdp')
All inputs are finite; a program needn't handle non-finite values.
Results may differ from a plain program's by a relative error of at most 0.0049.
Values may be sent and summed in bfloat16 or wider, within the bound.
A program may use at most 32 MiB of HBM per device.

v0:
```python
import math

import jax
import jax.numpy as jnp
from jax import lax
from jax.sharding import PartitionSpec as P


def summed_rows(operand, weight, transposed):

    def piece_term():
        if transposed:
            return lax.dot_general(
                operand, weight, (((1,), (1,)), ((), ())), preferred_element_type=jnp.float32
            )
        return jnp.dot(operand, weight, preferred_element_type=jnp.float32)

    return lax.psum_scatter(piece_term(), "fsdp", scatter_dimension=0, tiled=True)


def width_rows(partial_value):
    return lax.psum_scatter(partial_value, "tp", scatter_dimension=0, tiled=True)


def spread_hidden(shard, weight, partner, transposed):
    if transposed:
        grad_init = jnp.zeros((partner.shape[1], shard.shape[1]), jnp.float32)
    else:
        grad_init = jnp.zeros((shard.shape[1], partner.shape[1]), jnp.float32)
    shard_piece = lax.all_gather(shard, "fsdp", axis=0, tiled=True)
    grad_sum = grad_init
    if transposed:
        product = lax.dot_general(
            shard_piece, weight, (((1,), (1,)), ((), ())), preferred_element_type=jnp.float32
        )
    else:
        product = jnp.dot(shard_piece, weight, preferred_element_type=jnp.float32)
    if transposed:
        grad_sum = lax.dot_general(
            partner, shard_piece, (((0,), (0,)), ((), ())), preferred_element_type=jnp.float32
        )
    else:
        grad_sum = lax.dot_general(
            shard_piece, partner, (((0,), (0,)), ((), ())), preferred_element_type=jnp.float32
        )
    return (product, grad_sum)


def body(tokens, up_weight, down_weight, out_grad):
    gathered, grad_rows = (
        lax.all_gather(tokens, "tp", axis=0, tiled=True),
        lax.all_gather(out_grad, "tp", axis=0, tiled=True),
    )
    row_total = gathered.shape[0]
    grad_scale = 1.0 / math.sqrt(row_total)
    pre_own = summed_rows(gathered, up_weight, False)
    hidden_own = jax.nn.gelu(pre_own).astype(jnp.bfloat16)
    out_part, down_sum = spread_hidden(hidden_own, down_weight, grad_rows, False)
    output = width_rows(out_part).astype(jnp.bfloat16)
    back_own = summed_rows(grad_rows, down_weight, True)
    unused, pull_back = jax.vjp(jax.nn.gelu, pre_own)
    local_slope = pull_back(back_own)[0].astype(jnp.bfloat16)
    in_part, up_sum = spread_hidden(local_slope, up_weight, gathered, True)
    in_grad = width_rows(in_part).astype(jnp.bfloat16)
    up_grad = (up_sum * grad_scale).astype(jnp.bfloat16)
    down_grad = (down_sum * grad_scale).astype(jnp.bfloat16)
    return (output, in_grad, up_grad, down_grad)


def solution(mesh):
    return jax.shard_map(
        body,
        mesh=mesh,
        in_specs=(P("tp", "fsdp"), P("fsdp", "tp"), P("tp", "fsdp"), P("tp", "fsdp")),
        out_specs=(P("tp", "fsdp"), P("tp", "fsdp"), P("fsdp", "tp"), P("tp", "fsdp")),
        check_vma=False,
    )
```

profile of v0, /device:TPU:2, one launch (start us, length us, event | category | flops | bytes accessed | tf_op | source)
XLA Modules:
  0.0 642.1 jit_solution(6416055568164001404)
XLA Ops:
  7.2 0.0 copy-start
  7.2 0.0 reduce-scatter.9.cloned.1.call-start
  7.2 78.2 %all_gather.14 = bf16[512,384]{1,0:T(8,128)(2,1)S(1)} all-gather(bf16[16,384]{1,0:T(8,128)(2,1)} %param.7), channel_id=1, replica_groups=mesh['fsdp'=32,'tp'=32] {'tp'}, dimensions={0}, use_global_device_ids=true | all-gather | bytes 405504 | tf_op jit(solution)/shard_map/all_gather | solution.py:52
  85.4 0.0 copy-start.2
  85.5 0.8 copy-done.2
  86.2 3.0 fusion.12
  89.2 0.0 copy-start.5
  89.2 0.0 reduce-scatter.9.cloned.1.call-update
  89.3 0.0 reduce-scatter.5.cloned.1.call-start
  89.3 0.6 copy-done.5
  89.9 60.4 %all_gather.12 = bf16[512,384]{1,0:T(8,128)(2,1)S(1)} all-gather(bf16[16,384]{1,0:T(8,128)(2,1)S(1)} %copy-done.5), channel_id=1, replica_groups=mesh['fsdp'=32,'tp'=32] {'tp'}, dimensions={0}, use_global_device_ids=true | all-gather | bytes 405504 | tf_op jit(solution)/shard_map/all_gather | solution.py:51
  150.4 0.0 copy-start.4
  150.4 0.7 copy-done.4
  151.1 0.0 copy-done
  151.1 1.9 fusion.10
  153.0 0.0 reduce-scatter.5.cloned.1.call-update
  153.1 0.0 reduce-scatter.11.cloned.1.call-start
  153.1 40.9 %reduce-scatter.9.cloned.1.call-done = f32[16,896]{1,0:T(8,128)} async-done(((f32[512,896]{1,0:T(8,128)}), f32[16,896]{1,0:T(8,128)}) %reduce-scatter.9.cloned.1.call-update) | async-done | bytes 57360 | tf_op jit(solution)/shard_map/reduce_scatter | solution.py:18
  194.0 119.3 %reduce-scatter.5.cloned.1.call-done = f32[16,896]{1,0:T(8,128)} async-done(((f32[512,896]{1,0:T(8,128)}), f32[16,896]{1,0:T(8,128)}) %reduce-scatter.5.cloned.1.call-update) | async-done | bytes 57360 | tf_op jit(solution)/shard_map/reduce_scatter | solution.py:18
  313.3 0.9 fusion.9
  314.2 43.9 %all_gather.15 = bf16[512,896]{1,0:T(8,128)(2,1)S(1)} all-gather(bf16[16,896]{1,0:T(8,128)(2,1)S(1)} %get-tuple-element.8), channel_id=1, replica_groups=mesh['fsdp'=32,'tp'=32] {'fsdp'}, dimensions={0}, use_global_device_ids=true | all-gather | bytes 946176 | tf_op jit(solution)/shard_map/all_gather | solution.py:30
  358.1 1.6 fusion.13
  359.6 0.0 copy-start.1
  359.6 0.0 reduce-scatter.11.cloned.1.call-update
  359.7 0.0 reduce-scatter.7.cloned.1.call-start
  359.7 45.4 %all_gather.13 = bf16[512,896]{1,0:T(8,128)(2,1)S(1)} all-gather(bf16[16,896]{1,0:T(8,128)(2,1)S(1)} %get-tuple-element.9), channel_id=1, replica_groups=mesh['fsdp'=32,'tp'=32] {'fsdp'}, dimensions={0}, use_global_device_ids=true | all-gather | bytes 946176 | tf_op jit(solution)/shard_map/all_gather | solution.py:30
  405.1 0.0 copy-done.1
  405.1 1.5 fusion.11
  406.6 0.0 reduce-scatter.7.cloned.1.call-update
  406.7 0.0 copy-start.3
  406.7 2.6 fusion.2
  409.2 2.2 copy.8
  411.5 0.0 copy-done.3
  411.5 1.5 fusion.1
  413.0 87.2 %reduce-scatter.11.cloned.1.call-done = f32[16,384]{1,0:T(8,128)} async-done(((f32[512,384]{1,0:T(8,128)}), f32[16,384]{1,0:T(8,128)}) %reduce-scatter.11.cloned.1.call-update) | async-done | bytes 24592 | tf_op jit(solution)/shard_map/reduce_scatter | solution.py:22
  500.2 1.3 convert_element_type.24
  501.5 132.7 %reduce-scatter.7.cloned.1.call-done = f32[16,384]{1,0:T(8,128)} async-done(((f32[512,384]{1,0:T(8,128)}), f32[16,384]{1,0:T(8,128)}) %reduce-scatter.7.cloned.1.call-update) | async-done | bytes 24592 | tf_op jit(solution)/shard_map/reduce_scatter | solution.py:22
  634.3 1.3 convert_element_type.22
Async XLA Ops:
  7.2 144.0 %copy-start = (bf16[384,896]{1,0:T(8,128)(2,1)S(1)}, bf16[384,896]{1,0:T(8,128)(2,1)}, u32[]{:S(2)}) copy-start(bf16[384,896]{1,0:T(8,128)(2,1)} %param.5) | copy-start | bytes 2064388
  7.2 186.8 %reduce-scatter.9.cloned.1.call-start = ((), (), s32[]{:S(2)}) async-start(), calls=%async_computation.6 | async-start | bytes 1892352 | tf_op jit(solution)/shard_map/reduce_scatter | solution.py:18
  85.4 0.8 copy-start.2
  89.2 0.7 copy-start.5
  89.3 224.0 %reduce-scatter.5.cloned.1.call-start = ((), (), s32[]{:S(2)}) async-start(), calls=%async_computation.4 | async-start | bytes 1892352 | tf_op jit(solution)/shard_map/reduce_scatter | solution.py:18
  150.4 0.7 copy-start.4
  153.1 347.1 %reduce-scatter.11.cloned.1.call-start = ((), (), s32[]{:S(2)}) async-start(), calls=%async_computation.7 | async-start | bytes 811008 | tf_op jit(solution)/shard_map/reduce_scatter | solution.py:22
  359.6 45.4 %copy-start.1 = (bf16[896,384]{1,0:T(8,128)(2,1)S(1)}, bf16[896,384]{1,0:T(8,128)(2,1)}, u32[]{:S(2)}) copy-start(bf16[896,384]{1,0:T(8,128)(2,1)} %param.6) | copy-start | bytes 2064388
  359.7 274.6 %reduce-scatter.7.cloned.1.call-start = ((), (), s32[]{:S(2)}) async-start(), calls=%async_computation.5 | async-start | bytes 811008 | tf_op jit(solution)/shard_map/reduce_scatter | solution.py:22
  406.7 4.8 copy-start.3
Sparse Core Ops, SparseCore 0:
  89.4 104.5 reduce-scatter.8
  199.6 113.6 reduce-scatter.4
  359.8 140.3 reduce-scatter.10
  503.8 130.4 reduce-scatter.6
where the time goes:
time: 643 us; the launch traced here: 642 us
  waiting for transfers between devices  380 us (59%)
  blocking collectives  228 us (35%)
  between operations  13.8 us (2%)
  matrix products  12.1 us (2%)
    reduce_scatter x2, waiting for transfers between devices, width_rows(): lax.psum_scatter(partial_value, 'tp', scatter_dimension=0, tiled=True)  220 us
    reduce_scatter x2, waiting for transfers between devices, summed_rows(): lax.psum_scatter(piece_term(), 'fsdp', scatter_dimension=0, tiled=True)  160 us
    all_gather x2, blocking collectives, spread_hidden(): shard_piece = lax.all_gather(shard, 'fsdp', axis=0, tiled=True)  89.2 us
    all_gather x1, blocking collectives, body(): lax.all_gather(out_grad, 'tp', axis=0, tiled=True)  78.2 us
    all_gather x1, blocking collectives, body(): lax.all_gather(tokens, 'tp', axis=0, tiled=True)  60.4 us
  transfers between devices with their start and end apart: 4, of which 4 were waited for; matrix products, arithmetic and copies ran while one was open for 2% of the time, Pallas kernels for 0%

commit v1 on v0

v1 whole, which is shorter than its diff:
```python
import functools
import math

import jax
import jax.numpy as jnp
from jax import lax
from jax.experimental import pallas as pl
from jax.experimental.pallas import tpu as pltpu
from jax.sharding import PartitionSpec as P

MESH = pl.DeviceIdType.MESH
BF16 = jnp.bfloat16
F32 = jnp.float32

NX, NYH, NYL, NZ = 4, 4, 2, 16
ROWS = 16
HALF = NZ * ROWS
TOKENS = NYL * HALF
FEAT, HID = 384, 896
CUT = 512
N_SEM = 288
LEAD = 6
GELU_A = math.sqrt(2.0 / math.pi)
GELU_B = 0.044715


def gelu(v):
    return 0.5 * v * (1.0 + jnp.tanh(GELU_A * (v + GELU_B * v * v * v)))


def gelu_slope(v):
    t = jnp.tanh(GELU_A * (v + GELU_B * v * v * v))
    return 0.5 * (1.0 + t) + 0.5 * v * (1.0 - t * t) * GELU_A * (1.0 + 3.0 * GELU_B * v * v)


def dot(a, b, ca=1, cb=0):
    return lax.dot_general(a, b, (((ca,), (cb,)), ((), ())), preferred_element_type=F32)


def kernel(
    tok, up, down, cot, out, in_grad, up_grad, down_grad,
    t0, t1, s0, s1, wu, wd, p0, p1, sx, rx, ry0, ry1, pre_ref, h0, h1,
    ob, rb, sum0, sum1, rz, du, dd, send_sem, recv_sem, local_sem,
):
    f = lax.axis_index("fsdp")
    t = lax.axis_index("tp")
    c = lax.rem(f, 2)
    x = lax.rem(f // 2, NX)
    yh = f // (2 * NX)
    yl = t // NZ
    z = lax.rem(t, NZ)

    def dev(x_=None, yh_=None, c_=None, yl_=None, z_=None):
        x_ = x if x_ is None else x_
        yh_ = yh if yh_ is None else yh_
        c_ = c if c_ is None else c_
        yl_ = yl if yl_ is None else yl_
        z_ = z if z_ is None else z_
        return ((yh_ * NX + x_) * 2 + c_, yl_ * NZ + z_)

    def mod(v, n):
        return lax.rem(v + n, n)

    xp, xm, xo = mod(x + 1, NX), mod(x - 1, NX), mod(x + 2, NX)
    yp, ym, yo = mod(yh + 1, NYH), mod(yh - 1, NYH), mod(yh + 2, NYH)
    sibling, partner = dev(c_=1 - c), dev(yl_=1 - yl)
    x_up, x_down = dev(x_=xp), dev(x_=xm)
    y_up, y_down = dev(yh_=yp), dev(yh_=ym)
    z_up, z_down = dev(z_=mod(z + 1, NZ)), dev(z_=mod(z - 1, NZ))

    pending = []
    used = [0, 0]

    def local(src, dst):
        copy = pltpu.make_async_copy(src, dst, local_sem.at[used[1]])
        used[1] += 1
        copy.start()
        return copy

    def send(src, dst, to):
        copy = pltpu.make_async_remote_copy(
            src_ref=src, dst_ref=dst, send_sem=send_sem.at[used[0]], recv_sem=recv_sem.at[used[0]],
            device_id=to, device_id_type=MESH,
        )
        used[0] += 1
        copy.start()
        pending.append(copy)
        return copy

    def zrows(k):
        return pl.ds(pl.multiple_of(mod(z + k, NZ) * ROWS, ROWS), ROWS)

    weights = [local(up, wu.at[0]), local(down, wd.at[0])]
    own_rows = [
        local(src, buf.at[yl, zrows(0), :]) for src, buf in ((tok, t0), (cot, t1))
    ]

    barrier = pltpu.get_barrier_semaphore()
    peers = (sibling, partner, x_up, x_down, y_up, y_down, z_up, z_down)
    for peer in peers:
        pl.semaphore_signal(barrier, inc=1, device_id=peer, device_id_type=MESH)
    pl.semaphore_wait(barrier, len(peers))

    done = set()
    weight_copies = []

    def chain(a):
        src, rows_all, rows_sib, part, h, total, result = (
            (tok, t0, s0, p0, h0, sum0, out), (cot, t1, s1, p1, h1, sum1, in_grad)
        )[a]
        long, short = ((z_up, z_down), (z_down, z_up))[a]
        sign = (1, -1)[a]

        first = send(src, rows_all.at[yl, zrows(0), :], partner)
        yield
        forwards = []

        def forward(k):
            forwards.append(send(rows_all.at[1 - c, zrows(k), :], rows_sib.at[zrows(k), :], sibling))

        own_rows[a].wait()
        first.wait_recv()
        to_forward = [0]
        for hop in range(NZ // 2):
            k = -sign * hop
            one = send(rows_all.at[:, zrows(k), :], rows_all.at[:, zrows(k), :], long)
            two = None
            if hop < NZ // 2 - 1:
                two = send(rows_all.at[:, zrows(-k), :], rows_all.at[:, zrows(-k), :], short)
            for k_ in to_forward:
                forward(k_)
            if a == 0 and hop == 0:
                weight_copies.extend((send(up, wu.at[1], sibling), send(down, wd.at[1], sibling)))
            yield
            one.wait_recv()
            to_forward = [k - sign]
            if two is not None:
                two.wait_recv()
                to_forward.append(-k + sign)
        for k_ in to_forward:
            forward(k_)
        done.add(("rows", a))
        yield
        for copy in forwards:
            copy.wait_recv()

        if a == 0:
            weights[0].wait()
            weight_copies[0].wait_recv()
            part[...] = dot(rows_all[c], wu[0]) + dot(rows_sib[...], wu[1])
        else:
            weights[1].wait()
            weight_copies[1].wait_recv()
            part[...] = dot(rows_all[c], wd[0], 1, 1) + dot(rows_sib[...], wd[1], 1, 1)

        def xrows(x_, half):
            return pl.ds(pl.multiple_of(x_ * 64 + half * 32, 32), 32)

        def put(k, x_, half, to, add=None):
            value = part[xrows(x_, half), :]
            if add is not None:
                value = value + rx[a, add].astype(F32)
            sx[a, k] = value.astype(BF16)
            return send(sx.at[a, k], rx.at[a, k], to)

        m0 = put(0, xo, 0, x_up)
        m1 = put(1, xo, 1, x_down)
        m2 = put(2, xp, 1, x_up)
        m3 = put(3, xm, 0, x_down)
        yield
        m0.wait_recv()
        m4 = put(4, xp, 0, x_up, 0)
        m1.wait_recv()
        m5 = put(5, xm, 1, x_down, 1)
        yield
        m3.wait_recv()
        m2.wait_recv()
        m4.wait_recv()
        part[xrows(x, 0), :] += rx[a, 3].astype(F32) + rx[a, 4].astype(F32)
        m5.wait_recv()
        part[xrows(x, 1), :] += rx[a, 2].astype(F32) + rx[a, 5].astype(F32)

        def yrows(y_):
            return pl.ds(pl.multiple_of(x * 64 + y_ * ROWS, ROWS), ROWS)

        lo, hi = pl.ds(0, CUT), pl.ds(CUT, HID - CUT)
        n0 = send(part.at[yrows(yo), lo], ry0.at[a, 0], y_up)
        n1 = send(part.at[yrows(yo), hi], ry1.at[a, 0], y_down)
        n2 = send(part.at[yrows(yp), hi], ry1.at[a, 1], y_up)
        n3 = send(part.at[yrows(ym), lo], ry0.at[a, 1], y_down)
        yield
        n0.wait_recv()
        part[yrows(yp), lo] += ry0[a, 0]
        n4 = send(part.at[yrows(yp), lo], ry0.at[a, 2], y_up)
        n1.wait_recv()
        part[yrows(ym), hi] += ry1[a, 0]
        n5 = send(part.at[yrows(ym), hi], ry1.at[a, 2], y_down)
        yield
        n2.wait_recv()
        n3.wait_recv()
        n4.wait_recv()
        n5.wait_recv()
        part[yrows(yh), lo] += ry0[a, 1] + ry0[a, 2]
        part[yrows(yh), hi] += ry1[a, 1] + ry1[a, 2]

        def hrows(x_, y_):
            return pl.ds(pl.multiple_of(c * HALF + x_ * 64 + y_ * ROWS, ROWS), ROWS)

        value = part[yrows(yh), :]
        if a == 0:
            pre_ref[...] = value
            h[hrows(x, yh), :] = gelu(value).astype(BF16)
            done.add("pre")
        else:
            assert "pre" in done
            h[hrows(x, yh), :] = (value * gelu_slope(pre_ref[...])).astype(BF16)

        def block(x_, y_, to, cols=None):
            ref = h.at[hrows(x_, y_), :] if cols is None else h.at[hrows(x_, y_), cols]
            return send(ref, ref, to)

        def column(x_):
            rows = pl.ds(pl.multiple_of(c * HALF + x_ * 64, 64), 64)
            return send(h.at[rows, :], h.at[rows, :], sibling)

        ya, yb = block(x, yh, y_up), block(x, yh, y_down)
        xa0, xb0 = block(x, yh, x_up), block(x, yh, x_down)
        yield
        ya.wait_recv()
        yc = block(x, ym, y_up, lo)
        xa1, xb1 = block(x, ym, x_up), block(x, ym, x_down)
        yb.wait_recv()
        yd = block(x, yp, y_down, hi)
        xa2, xb2 = block(x, yp, x_up), block(x, yp, x_down)
        yield
        xa0.wait_recv()
        relays = [block(xm, yh, x_up)]
        yc.wait_recv()
        yd.wait_recv()
        xa3, xb3 = block(x, yo, x_up), block(x, yo, x_down)
        columns = [column(x)]
        yield
        xa1.wait_recv()
        relays.append(block(xm, ym, x_up))
        xb2.wait_recv()
        relays.append(block(xp, yp, x_down))
        yield
        xb3.wait_recv()
        relays.append(block(xp, yo, x_down))
        xb0.wait_recv()
        xb1.wait_recv()
        columns.append(column(xp))
        xa2.wait_recv()
        xa3.wait_recv()
        columns.append(column(xm))
        yield
        for copy in relays:
            copy.wait_recv()
        columns.append(column(xo))
        yield
        for copy in columns:
            copy.wait_recv()
        done.add(("hidden", a))

        def product(half):
            rows = h[pl.ds(pl.multiple_of(half * HALF, HALF), HALF), :]
            return dot(rows, wd[0]) if a == 0 else dot(rows, wu[0], 1, 1)

        ob[a] = product(1 - yl).astype(BF16)
        order = [sign * (NZ // 2)]
        for k in range(NZ // 2 - 1, 0, -1):
            order += [sign * k, -sign * k]
        order.append(0)
        across = {}
        for k in order:
            across[k] = send(ob.at[a, zrows(k), :], rb.at[a, zrows(k), :], partner)
        total[...] = product(yl)

        one = two = None
        for hop in range(NZ // 2):
            yield
            k = sign * (NZ // 2 - hop)
            across[k].wait_recv()
            value = total[zrows(k), :] + rb[a, zrows(k), :].astype(F32)
            if one is not None:
                one.wait_recv()
                value = value + rz[a, hop - 1]
            total[zrows(k), :] = value
            one = send(total.at[zrows(k), :], rz.at[a, hop], long)
            if hop >= 1:
                across[-k].wait_recv()
                value = total[zrows(-k), :] + rb[a, zrows(-k), :].astype(F32)
                if two is not None:
                    two.wait_recv()
                    value = value + rz[a, NZ // 2 + hop - 2]
                total[zrows(-k), :] = value
                two = send(total.at[zrows(-k), :], rz.at[a, NZ // 2 + hop - 1], short)
        yield
        across[0].wait_recv()
        value = total[zrows(0), :] + rb[a, zrows(0), :].astype(F32)
        one.wait_recv()
        two.wait_recv()
        value = value + (rz[a, NZ // 2 - 1] + rz[a, NZ - 2])
        result[...] = value.astype(BF16)

    scale = 1.0 / math.sqrt(TOKENS)
    grads = []

    def down_product():
        dd[...] = (dot(h0[...], t1[...].reshape(TOKENS, FEAT), 0, 0) * scale).astype(BF16)
        grads.append(local(dd, down_grad))

    def up_product():
        du[...] = (dot(t0[...].reshape(TOKENS, FEAT), h1[...], 0, 0) * scale).astype(BF16)
        grads.append(local(du, up_grad))

    forward_chain, backward_chain = chain(0), chain(1)
    live = [True, True]
    todo = [down_product, up_product]

    def advance(which, gen):
        if live[which] and next(gen, "end") == "end":
            live[which] = False

    step = 0
    while any(live):
        advance(0, forward_chain)
        if step >= LEAD:
            advance(1, backward_chain)
        step += 1
        for index, need in ((0, (("hidden", 0), ("rows", 1))), (1, (("hidden", 1),))):
            if todo[index] is not None and all(n in done for n in need):
                todo[index]()
                todo[index] = None
                break

    assert all(job is None for job in todo)
    for copy in pending:
        copy.wait_send()
    for copy in grads:
        copy.wait()


def body(tokens, up_weight, down_weight, out_grad):
    anywhere = pl.BlockSpec(memory_space=pl.ANY)
    vmem = pl.BlockSpec(memory_space=pltpu.VMEM)
    return pl.pallas_call(
        kernel,
        out_shape=(
            jax.ShapeDtypeStruct((ROWS, FEAT), BF16),
            jax.ShapeDtypeStruct((ROWS, FEAT), BF16),
            jax.ShapeDtypeStruct((FEAT, HID), BF16),
            jax.ShapeDtypeStruct((HID, FEAT), BF16),
        ),
        in_specs=[anywhere] * 4,
        out_specs=(vmem, vmem, anywhere, anywhere),
        scratch_shapes=[
            pltpu.VMEM((NYL, HALF, FEAT), BF16),
            pltpu.VMEM((NYL, HALF, FEAT), BF16),
            pltpu.VMEM((HALF, FEAT), BF16),
            pltpu.VMEM((HALF, FEAT), BF16),
            pltpu.VMEM((2, FEAT, HID), BF16),
            pltpu.VMEM((2, HID, FEAT), BF16),
            pltpu.VMEM((HALF, HID), F32),
            pltpu.VMEM((HALF, HID), F32),
            pltpu.VMEM((2, 6, 32, HID), BF16),
            pltpu.VMEM((2, 6, 32, HID), BF16),
            pltpu.VMEM((2, 3, ROWS, CUT), F32),
            pltpu.VMEM((2, 3, ROWS, HID - CUT), F32),
            pltpu.VMEM((ROWS, HID), F32),
            pltpu.VMEM((TOKENS, HID), BF16),
            pltpu.VMEM((TOKENS, HID), BF16),
            pltpu.VMEM((2, HALF, FEAT), BF16),
            pltpu.VMEM((2, HALF, FEAT), BF16),
            pltpu.VMEM((HALF, FEAT), F32),
            pltpu.VMEM((HALF, FEAT), F32),
            pltpu.VMEM((2, NZ - 1, ROWS, FEAT), F32),
            pltpu.VMEM((FEAT, HID), BF16),
            pltpu.VMEM((HID, FEAT), BF16),
            pltpu.SemaphoreType.DMA((N_SEM,)),
            pltpu.SemaphoreType.DMA((N_SEM,)),
            pltpu.SemaphoreType.DMA((8,)),
        ],
        compiler_params=pltpu.CompilerParams(
            collective_id=0, has_side_effects=True, vmem_limit_bytes=48 * 1024 * 1024
        ),
    )(tokens, up_weight, down_weight, out_grad)


def solution(mesh):
    return jax.shard_map(
        body,
        mesh=mesh,
        in_specs=(P("tp", "fsdp"), P("fsdp", "tp"), P("tp", "fsdp"), P("tp", "fsdp")),
        out_specs=(P("tp", "fsdp"), P("tp", "fsdp"), P("fsdp", "tp"), P("tp", "fsdp")),
        check_vma=False,
    )
```

time: 643 us -> 150 us (0.23)
  the two profiles are of different devices: /device:TPU:2 before, /device:TPU:22 now
where the time goes in v1:
time: 150 us
  Pallas kernels  143 us (95%)
  local copies, waits for them, and re-layouts  6.5 us (4%)
    pallas_call x1, Pallas kernels, body(): pl.pallas_call(kernel, out_shape=(jax.ShapeDtypeStruct((ROWS, FEAT), BF16...  143 us
    unnamed x12, local copies, waits for them, and re-layouts  6.5 us

profile of v1, /device:TPU:22, one launch (start us, length us, event | category | flops | bytes accessed | tf_op | source)
XLA Modules:
  0.0 149.9 jit_solution(6150756732121583569)
XLA Ops:
  0.6 0.0 copy-start
  0.6 1.1 copy-done
  1.7 0.0 copy-start.1
  1.7 1.1 copy-done.1
  2.8 0.0 copy-start.2
  2.8 0.7 copy-done.2
  3.5 0.0 copy-start.3
  3.5 0.7 copy-done.3
  4.2 142.7 %shard_map.75 = (bf16[16,384]{1,0:T(8,128)(2,1)S(1)}, bf16[16,384]{1,0:T(8,128)(2,1)S(1)}, bf16[384,896]{1,0:T(8,128)(2,1)S(1)}, bf16[896,384]{1,0:T(8,128)(2,1)S(1)}) custom-call(bf16[16,384]{1,0:T(8,128)(2,1)S(1)} %copy-done.2, bf16[384,896]{1,0:T(8,128)(2,1)S(1)} %copy-done, bf16[896,384]{1,0:T(8,128)(2,1)S(1)} %copy-done.1, bf16[16,384]{1,0:T(8,128)(2,1)S(1)} %copy-done.3), custom_call_target="tpu_custom_call" | custom-call | tf_op jit(solution)/shard_map/pallas_call | solution.py:347
  147.0 0.6 copy.12
  147.6 0.6 copy.13
  148.2 0.8 copy.14
  149.0 0.8 copy.15
Async XLA Ops:
  0.6 1.1 copy-start
  1.7 1.1 copy-start.1
  2.8 0.7 copy-start.2
  3.5 0.7 copy-start.3

commit v2 on v1

v2 whole, which is shorter than its diff:
```python
import functools
import math

import jax
import jax.numpy as jnp
from jax import lax
from jax.experimental import pallas as pl
from jax.experimental.pallas import tpu as pltpu
from jax.sharding import PartitionSpec as P

MESH = pl.DeviceIdType.MESH
BF16 = jnp.bfloat16
F32 = jnp.float32

NX, NYH, NYL, NZ = 4, 4, 2, 16
ROWS = 16
HALF = NZ * ROWS
TOKENS = NYL * HALF
FEAT, HID = 384, 896
AWAY = (2, 1, -1)
Z_AWAY = (8,) + tuple(s * k for k in range(7, 0, -1) for s in (1, -1))
N_SEM = 176
ORDER = "FBFFBFBFBFBFBFBFBGBGFB"
GELU_A = math.sqrt(2.0 / math.pi)
GELU_B = 0.044715


def gelu(v):
    return 0.5 * v * (1.0 + jnp.tanh(GELU_A * (v + GELU_B * v * v * v)))


def gelu_slope(v):
    t = jnp.tanh(GELU_A * (v + GELU_B * v * v * v))
    return 0.5 * (1.0 + t) + 0.5 * v * (1.0 - t * t) * GELU_A * (1.0 + 3.0 * GELU_B * v * v)


def dot(a, b, ca=1, cb=0):
    return lax.dot_general(a, b, (((ca,), (cb,)), ((), ())), preferred_element_type=F32)


def kernel(
    tok, up, down, cot, out, in_grad, up_grad, down_grad,
    t0, t1, s0, s1, wu, wd, p0, p1, sx, rx, ry, pre_ref, h0, h1,
    ob, rb, sum0, sum1, zs, rz, du, dd, send_sem, recv_sem, local_sem,
):
    f = lax.axis_index("fsdp")
    t = lax.axis_index("tp")
    c = lax.rem(f, 2)
    x = lax.rem(f // 2, NX)
    yh = f // (2 * NX)
    yl = t // NZ
    z = lax.rem(t, NZ)

    def dev(x_=None, yh_=None, c_=None, yl_=None, z_=None):
        x_ = x if x_ is None else x_
        yh_ = yh if yh_ is None else yh_
        c_ = c if c_ is None else c_
        yl_ = yl if yl_ is None else yl_
        z_ = z if z_ is None else z_
        return ((yh_ * NX + x_) * 2 + c_, yl_ * NZ + z_)

    def mod(v, n):
        return lax.rem(v + n, n)

    sibling, partner = dev(c_=1 - c), dev(yl_=1 - yl)
    x_peers = [mod(x + k, NX) for k in AWAY]
    y_peers = [mod(yh + k, NYH) for k in AWAY]
    x_devs = [dev(x_=v) for v in x_peers]
    y_devs = [dev(yh_=v) for v in y_peers]
    z_devs = [dev(z_=mod(z + k, NZ)) for k in Z_AWAY]

    pending = []
    used = [0, 0]

    def local(src, dst):
        copy = pltpu.make_async_copy(src, dst, local_sem.at[used[1]])
        used[1] += 1
        copy.start()
        return copy

    def send(src, dst, to):
        copy = pltpu.make_async_remote_copy(
            src_ref=src, dst_ref=dst, send_sem=send_sem.at[used[0]], recv_sem=recv_sem.at[used[0]],
            device_id=to, device_id_type=MESH,
        )
        used[0] += 1
        copy.start()
        pending.append(copy)
        return copy

    def zrows(k):
        return pl.ds(pl.multiple_of(mod(z + k, NZ) * ROWS, ROWS), ROWS)

    weights = [local(up, wu.at[0]), local(down, wd.at[0])]
    own_rows = [
        local(src, buf.at[yl, zrows(0), :]) for src, buf in ((tok, t0), (cot, t1))
    ]

    barrier = pltpu.get_barrier_semaphore()
    peers = (sibling, partner, *x_devs, *y_devs, *z_devs)
    for peer in peers:
        pl.semaphore_signal(barrier, inc=1, device_id=peer, device_id_type=MESH)
    pl.semaphore_wait(barrier, len(peers))

    done = set()
    weight_copies = []

    def chain(a):
        src, rows_all, rows_sib, part, h, total, result = (
            (tok, t0, s0, p0, h0, sum0, out), (cot, t1, s1, p1, h1, sum1, in_grad)
        )[a]

        mine = rows_all.at[yl, zrows(0), :]
        over_z = [send(src, mine, to) for to in z_devs]
        over_y = [send(src, mine, partner)]
        if a == 0:
            weight_copies.extend((send(up, wu.at[1], sibling), send(down, wd.at[1], sibling)))
        yield
        own_rows[a].wait()
        for k, copy in reversed(tuple(zip(Z_AWAY, over_z))):
            copy.wait_recv()
            there = rows_all.at[yl, zrows(-k), :]
            over_y.append(send(there, there, partner))
        yield
        for copy in over_y:
            copy.wait_recv()
        across = send(rows_all.at[1 - c], rows_sib, sibling)
        done.add(("rows", a))

        w, contract = ((wu, 0), (wd, 1))[a]
        weights[a].wait()
        part[...] = dot(rows_all[c], w[0], 1, contract)
        weight_copies[a].wait_recv()
        across.wait_recv()
        part[...] += dot(rows_sib[...], w[1], 1, contract)

        def xrows(x_):
            return pl.ds(pl.multiple_of(x_ * 64, 64), 64)

        copies = []
        for i, (there, to) in enumerate(zip(x_peers, x_devs)):
            sx[a, i] = part[xrows(there), :].astype(BF16)
            copies.append(send(sx.at[a, i], rx.at[a, i], to))
        yield
        for copy in copies:
            copy.wait_recv()
        part[xrows(x), :] += rx[a, 0].astype(F32) + rx[a, 1].astype(F32) + rx[a, 2].astype(F32)

        def yrows(y_):
            return pl.ds(pl.multiple_of(x * 64 + y_ * ROWS, ROWS), ROWS)

        copies = [
            send(part.at[yrows(there), :], ry.at[a, i], to)
            for i, (there, to) in enumerate(zip(y_peers, y_devs))
        ]
        yield
        for copy in copies:
            copy.wait_recv()
        value = part[yrows(yh), :] + (ry[a, 0] + ry[a, 1] + ry[a, 2])

        def hrows(x_, y_):
            return pl.ds(pl.multiple_of(c * HALF + x_ * 64 + y_ * ROWS, ROWS), ROWS)

        if a == 0:
            pre_ref[...] = value
            h[hrows(x, yh), :] = gelu(value).astype(BF16)
            done.add("pre")
        else:
            assert "pre" in done
            h[hrows(x, yh), :] = (value * gelu_slope(pre_ref[...])).astype(BF16)

        def block(y_, to):
            ref = h.at[hrows(x, y_), :]
            return send(ref, ref, to)

        def column(x_):
            rows = pl.ds(pl.multiple_of(c * HALF + x_ * 64, 64), 64)
            return send(h.at[rows, :], h.at[rows, :], sibling)

        over_yh = [block(yh, to) for to in y_devs]
        over_x = [[block(yh, to)] for to in x_devs]
        yield
        for i in (1, 2, 0):
            over_yh[i].wait_recv()
            for copies, to in zip(over_x, x_devs):
                copies.append(block(mod(yh - AWAY[i], NYH), to))
        columns = [column(x)]
        yield
        for i in (1, 2, 0):
            for copy in over_x[i]:
                copy.wait_recv()
            columns.append(column(mod(x - AWAY[i], NX)))
        yield
        for copy in columns:
            copy.wait_recv()
        done.add(("hidden", a))

        back, contract = ((wd, 0), (wu, 1))[a]

        def product(first, n):
            rows = h[pl.ds(pl.multiple_of(first, 128), n), :]
            return dot(rows, back[0], 1, contract)

        copies = []
        for i in range(2):
            rows = pl.ds(i * 128, 128)
            ob[a, rows, :] = product((1 - yl) * HALF + i * 128, 128).astype(BF16)
            copies.append(send(ob.at[a, rows, :], rb.at[a, rows, :], partner))
        total[...] = product(yl * HALF, HALF)
        yield
        for i, copy in enumerate(copies):
            rows = pl.ds(i * 128, 128)
            copy.wait_recv()
            total[rows, :] += rb[a, rows, :].astype(F32)

        zs[a] = total[...].astype(BF16)
        copies = [
            send(zs.at[a, zrows(k), :], rz.at[a, i], to)
            for i, (k, to) in enumerate(zip(Z_AWAY, z_devs))
        ]
        yield
        value = total[zrows(0), :]
        for i, copy in reversed(tuple(enumerate(copies))):
            copy.wait_recv()
            value = value + rz[a, i].astype(F32)
        result[...] = value.astype(BF16)

    scale = 1.0 / math.sqrt(TOKENS)
    grads = []

    def down_product():
        dd[...] = (dot(h0[...], t1[...].reshape(TOKENS, FEAT), 0, 0) * scale).astype(BF16)
        grads.append(local(dd, down_grad))

    def up_product():
        du[...] = (dot(t0[...].reshape(TOKENS, FEAT), h1[...], 0, 0) * scale).astype(BF16)
        grads.append(local(du, up_grad))

    steps = {
        "F": chain(0), "B": chain(1), "G": iter((down_product, up_product)),
    }
    for name in ORDER:
        step = next(steps[name], None)
        if step is not None:
            step()
    assert next(steps["F"], "end") == next(steps["B"], "end") == next(steps["G"], "end") == "end"

    for copy in pending:
        copy.wait_send()
    for copy in grads:
        copy.wait()


def body(tokens, up_weight, down_weight, out_grad):
    anywhere = pl.BlockSpec(memory_space=pl.ANY)
    vmem = pl.BlockSpec(memory_space=pltpu.VMEM)
    return pl.pallas_call(
        kernel,
        out_shape=(
            jax.ShapeDtypeStruct((ROWS, FEAT), BF16),
            jax.ShapeDtypeStruct((ROWS, FEAT), BF16),
            jax.ShapeDtypeStruct((FEAT, HID), BF16),
            jax.ShapeDtypeStruct((HID, FEAT), BF16),
        ),
        in_specs=[anywhere] * 4,
        out_specs=(vmem, vmem, anywhere, anywhere),
        scratch_shapes=[
            pltpu.VMEM((NYL, HALF, FEAT), BF16),
            pltpu.VMEM((NYL, HALF, FEAT), BF16),
            pltpu.VMEM((HALF, FEAT), BF16),
            pltpu.VMEM((HALF, FEAT), BF16),
            pltpu.VMEM((2, FEAT, HID), BF16),
            pltpu.VMEM((2, HID, FEAT), BF16),
            pltpu.VMEM((HALF, HID), F32),
            pltpu.VMEM((HALF, HID), F32),
            pltpu.VMEM((2, 3, 64, HID), BF16),
            pltpu.VMEM((2, 3, 64, HID), BF16),
            pltpu.VMEM((2, 3, ROWS, HID), F32),
            pltpu.VMEM((ROWS, HID), F32),
            pltpu.VMEM((TOKENS, HID), BF16),
            pltpu.VMEM((TOKENS, HID), BF16),
            pltpu.VMEM((2, HALF, FEAT), BF16),
            pltpu.VMEM((2, HALF, FEAT), BF16),
            pltpu.VMEM((HALF, FEAT), F32),
            pltpu.VMEM((HALF, FEAT), F32),
            pltpu.VMEM((2, HALF, FEAT), BF16),
            pltpu.VMEM((2, NZ - 1, ROWS, FEAT), BF16),
            pltpu.VMEM((FEAT, HID), BF16),
            pltpu.VMEM((HID, FEAT), BF16),
            pltpu.SemaphoreType.DMA((N_SEM,)),
            pltpu.SemaphoreType.DMA((N_SEM,)),
            pltpu.SemaphoreType.DMA((8,)),
        ],
        compiler_params=pltpu.CompilerParams(
            collective_id=0, has_side_effects=True, vmem_limit_bytes=60 * 1024 * 1024
        ),
    )(tokens, up_weight, down_weight, out_grad)


def solution(mesh):
    return jax.shard_map(
        body,
        mesh=mesh,
        in_specs=(P("tp", "fsdp"), P("fsdp", "tp"), P("tp", "fsdp"), P("tp", "fsdp")),
        out_specs=(P("tp", "fsdp"), P("tp", "fsdp"), P("fsdp", "tp"), P("tp", "fsdp")),
        check_vma=False,
    )
```

time: 150 us -> 107 us (0.71)
  the two profiles are of different devices: /device:TPU:22 before, /device:TPU:1 now
where the time goes in v2:
time: 107 us
  Pallas kernels  101 us (94%)
  local copies, waits for them, and re-layouts  4.84 us (5%)
    pallas_call x1, Pallas kernels, body(): pl.pallas_call(kernel, out_shape=(jax.ShapeDtypeStruct((ROWS, FEAT), BF16...  101 us
    unnamed x8, local copies, waits for them, and re-layouts  4.84 us

profile of v2, /device:TPU:1, one launch (start us, length us, event | category | flops | bytes accessed | tf_op | source)
XLA Modules:
  0.0 106.7 jit_solution(11824441834201302280)
XLA Ops:
  0.6 101.2 %shard_map.75 = (bf16[16,384]{1,0:T(8,128)(2,1)}, bf16[16,384]{1,0:T(8,128)(2,1)}, bf16[384,896]{1,0:T(8,128)(2,1)}, bf16[896,384]{1,0:T(8,128)(2,1)}) custom-call(bf16[16,384]{1,0:T(8,128)(2,1)} %tok.1, bf16[384,896]{1,0:T(8,128)(2,1)} %up.1, bf16[896,384]{1,0:T(8,128)(2,1)} %down.1, bf16[16,384]{1,0:T(8,128)(2,1)} %cot.1), custom_call_target="tpu_custom_call" | custom-call | tf_op jit(solution)/shard_map/pallas_call | solution.py:257
  101.8 0.0 copy-start.1
  101.8 1.3 %copy.12 = bf16[16,384]{1,0:T(8,128)(2,1)} copy(bf16[16,384]{1,0:T(8,128)(2,1)} %get-tuple-element.8) | data formatting | bytes 24576
  103.1 0.0 copy-done.1
  103.2 0.6 copy.13
  103.8 0.0 copy-start
  103.8 2.1 %copy.14 = bf16[384,896]{1,0:T(8,128)(2,1)} copy(bf16[384,896]{1,0:T(8,128)(2,1)} %get-tuple-element.10) | data formatting | bytes 1376256
  105.8 0.0 copy-done
  105.8 0.8 copy.15
Async XLA Ops:
  101.8 1.3 %copy-start.1 = (bf16[16,384]{1,0:T(8,128)(2,1)S(1)}, bf16[16,384]{1,0:T(8,128)(2,1)}, u32[]{:S(2)}) copy-start(bf16[16,384]{1,0:T(8,128)(2,1)} %get-tuple-element.9) | copy-start | bytes 36868
  103.8 2.1 %copy-start = (bf16[896,384]{1,0:T(8,128)(2,1)S(1)}, bf16[896,384]{1,0:T(8,128)(2,1)}, u32[]{:S(2)}) copy-start(bf16[896,384]{1,0:T(8,128)(2,1)} %get-tuple-element.11) | copy-start | bytes 2064388

commit v3 on v2

--- a/solution.py
+++ b/solution.py
@@ -19,8 +19,9 @@
 FEAT, HID = 384, 896
 AWAY = (2, 1, -1)
 Z_AWAY = (8,) + tuple(s * k for k in range(7, 0, -1) for s in (1, -1))
-N_SEM = 176
-ORDER = "FBFFBFBFBFBFBFBFBGBGFB"
+Z_DIRECT = (8, 6, -6, 3, -3, 1, -1)
+N_SEM = 208
+ORDER = "FBFBFFBFBFBFBFFBFBBGBGFB"
 GELU_A = math.sqrt(2.0 / math.pi)
 GELU_B = 0.044715
 
@@ -40,7 +41,7 @@
 
 def kernel(
     tok, up, down, cot, out, in_grad, up_grad, down_grad,
-    t0, t1, s0, s1, wu, wd, p0, p1, sx, rx, ry, pre_ref, h0, h1,
+    t0, t1, s0, s1, wu, wd, p0, p1, sx, rx, sy0, sy1, ry0, ry1, pre_ref, h0, h1,
     ob, rb, sum0, sum1, zs, rz, du, dd, send_sem, recv_sem, local_sem,
 ):
     f = lax.axis_index("fsdp")
@@ -67,7 +68,11 @@
     y_peers = [mod(yh + k, NYH) for k in AWAY]
     x_devs = [dev(x_=v) for v in x_peers]
     y_devs = [dev(yh_=v) for v in y_peers]
-    z_devs = [dev(z_=mod(z + k, NZ)) for k in Z_AWAY]
+
+    def z_dev(k):
+        return dev(z_=mod(z + k, NZ))
+
+    z_devs = [z_dev(k) for k in Z_AWAY]
 
     pending = []
     used = [0, 0]
@@ -111,16 +116,31 @@
         )[a]
 
         mine = rows_all.at[yl, zrows(0), :]
-        over_z = [send(src, mine, to) for to in z_devs]
+        direct = {k: send(src, mine, z_dev(k)) for k in Z_DIRECT}
         over_y = [send(src, mine, partner)]
         if a == 0:
             weight_copies.extend((send(up, wu.at[1], sibling), send(down, wd.at[1], sibling)))
         yield
-        own_rows[a].wait()
-        for k, copy in reversed(tuple(zip(Z_AWAY, over_z))):
-            copy.wait_recv()
+
+        def cross(k):
             there = rows_all.at[yl, zrows(-k), :]
             over_y.append(send(there, there, partner))
+
+        passed = {}
+        for k in (1, -1, 3, -3, 6, -6):
+            direct[k].wait_recv()
+            if abs(k) > 1:
+                there = rows_all.at[yl, zrows(-k), :]
+                for s in (1, -1):
+                    passed[k + s] = send(there, there, z_dev(s))
+            cross(k)
+        yield
+        direct[8].wait_recv()
+        cross(8)
+        for k, copy in passed.items():
+            copy.wait_recv()
+            cross(k)
+        own_rows[a].wait()
         yield
         for copy in over_y:
             copy.wait_recv()
@@ -137,26 +157,41 @@
         def xrows(x_):
             return pl.ds(pl.multiple_of(x_ * 64, 64), 64)
 
-        copies = []
-        for i, (there, to) in enumerate(zip(x_peers, x_devs)):
+        for i, there in enumerate(x_peers):
             sx[a, i] = part[xrows(there), :].astype(BF16)
-            copies.append(send(sx.at[a, i], rx.at[a, i], to))
-        yield
-        for copy in copies:
-            copy.wait_recv()
-        part[xrows(x), :] += rx[a, 0].astype(F32) + rx[a, 1].astype(F32) + rx[a, 2].astype(F32)
+        over_x = []
+        for there in y_peers + [yh]:
+            rows = pl.ds(pl.multiple_of(there * ROWS, ROWS), ROWS)
+            over_x.append(
+                [send(sx.at[a, i, rows, :], rx.at[a, i, rows, :], to) for i, to in enumerate(x_devs)]
+            )
+        yield
 
         def yrows(y_):
             return pl.ds(pl.multiple_of(x * 64 + y_ * ROWS, ROWS), ROWS)
 
-        copies = [
-            send(part.at[yrows(there), :], ry.at[a, i], to)
-            for i, (there, to) in enumerate(zip(y_peers, y_devs))
-        ]
-        yield
+        def sum_x(j, there):
+            for copy in over_x[j]:
+                copy.wait_recv()
+            rows = pl.ds(pl.multiple_of(there * ROWS, ROWS), ROWS)
+            got = rx[a, :, rows, :].astype(F32)
+            return part[yrows(there), :] + (got[0] + got[1] + got[2])
+
+        copies = []
+        for i, (there, to) in enumerate(zip(y_peers, y_devs)):
+            value = sum_x(i, there)
+            if a == 0:
+                sy0[i] = value.astype(BF16)
+                copies.append(send(sy0.at[i], ry0.at[i], to))
+            else:
+                sy1[i] = value
+                copies.append(send(sy1.at[i], ry1.at[i], to))
+        yield
+        value = sum_x(3, yh)
         for copy in copies:
             copy.wait_recv()
-        value = part[yrows(yh), :] + (ry[a, 0] + ry[a, 1] + ry[a, 2])
+        got = ry0[...].astype(F32) if a == 0 else ry1[...]
+        value = value + (got[0] + got[1] + got[2])
 
         def hrows(x_, y_):
             return pl.ds(pl.multiple_of(c * HALF + x_ * 64 + y_ * ROWS, ROWS), ROWS)
@@ -197,29 +232,25 @@
 
         back, contract = ((wd, 0), (wu, 1))[a]
 
-        def product(first, n):
-            rows = h[pl.ds(pl.multiple_of(first, 128), n), :]
+        def product(half):
+            rows = h[pl.ds(pl.multiple_of(half * HALF, HALF), HALF), :]
             return dot(rows, back[0], 1, contract)
 
+        ob[a] = product(1 - yl).astype(BF16)
+        across = [
+            send(ob.at[a, zrows(k), :], rb.at[a, zrows(k), :], partner) for k in Z_AWAY + (0,)
+        ]
+        total[...] = product(yl)
+        yield
+
         copies = []
-        for i in range(2):
-            rows = pl.ds(i * 128, 128)
-            ob[a, rows, :] = product((1 - yl) * HALF + i * 128, 128).astype(BF16)
-            copies.append(send(ob.at[a, rows, :], rb.at[a, rows, :], partner))
-        total[...] = product(yl * HALF, HALF)
-        yield
-        for i, copy in enumerate(copies):
-            rows = pl.ds(i * 128, 128)
-            copy.wait_recv()
-            total[rows, :] += rb[a, rows, :].astype(F32)
-
-        zs[a] = total[...].astype(BF16)
-        copies = [
-            send(zs.at[a, zrows(k), :], rz.at[a, i], to)
-            for i, (k, to) in enumerate(zip(Z_AWAY, z_devs))
-        ]
-        yield
-        value = total[zrows(0), :]
+        for i, (k, to) in enumerate(zip(Z_AWAY, z_devs)):
+            across[i].wait_recv()
+            zs[a, zrows(k), :] = (total[zrows(k), :] + rb[a, zrows(k), :].astype(F32)).astype(BF16)
+            copies.append(send(zs.at[a, zrows(k), :], rz.at[a, i], to))
+        across[-1].wait_recv()
+        yield
+        value = total[zrows(0), :] + rb[a, zrows(0), :].astype(F32)
         for i, copy in reversed(tuple(enumerate(copies))):
             copy.wait_recv()
             value = value + rz[a, i].astype(F32)
@@ -262,7 +293,7 @@
             jax.ShapeDtypeStruct((FEAT, HID), BF16),
             jax.ShapeDtypeStruct((HID, FEAT), BF16),
         ),
-        in_specs=[anywhere] * 4,
+        in_specs=[pl.BlockSpec(memory_space=pltpu.HBM)] * 4,
         out_specs=(vmem, vmem, anywhere, anywhere),
         scratch_shapes=[
             pltpu.VMEM((NYL, HALF, FEAT), BF16),
@@ -275,7 +306,10 @@
             pltpu.VMEM((HALF, HID), F32),
             pltpu.VMEM((2, 3, 64, HID), BF16),
             pltpu.VMEM((2, 3, 64, HID), BF16),
-            pltpu.VMEM((2, 3, ROWS, HID), F32),
+            pltpu.VMEM((3, ROWS, HID), BF16),
+            pltpu.VMEM((3, ROWS, HID), F32),
+            pltpu.VMEM((3, ROWS, HID), BF16),
+            pltpu.VMEM((3, ROWS, HID), F32),
             pltpu.VMEM((ROWS, HID), F32),
             pltpu.VMEM((TOKENS, HID), BF16),
             pltpu.VMEM((TOKENS, HID), BF16),

time: 107 us -> 97.8 us (0.914)
  Pallas kernels: 101 us -> 92.1 us
    pallas_call x1, Pallas kernels: 101 us -> 92.1 us  [body(): pl.pallas_call(kernel, out_shape=(jax.ShapeDtypeStruct((ROWS, FEAT), BF16...]
where the time goes in v3:
time: 97.8 us; the launch traced here: 97.6 us
  Pallas kernels  92.1 us (94%)
  local copies, waits for them, and re-layouts  4.84 us (5%)
    pallas_call x1, Pallas kernels, body(): pl.pallas_call(kernel, out_shape=(jax.ShapeDtypeStruct((ROWS, FEAT), BF16...  92.1 us
    unnamed x8, local copies, waits for them, and re-layouts  4.84 us

profile of v3, /device:TPU:1, one launch (start us, length us, event | category | flops | bytes accessed | tf_op | source)
XLA Modules:
  0.0 97.6 jit_solution(15366301658139979197)
XLA Ops:
  0.6 92.1 %shard_map.75 = (bf16[16,384]{1,0:T(8,128)(2,1)}, bf16[16,384]{1,0:T(8,128)(2,1)}, bf16[384,896]{1,0:T(8,128)(2,1)}, bf16[896,384]{1,0:T(8,128)(2,1)}) custom-call(bf16[16,384]{1,0:T(8,128)(2,1)} %tok.1, bf16[384,896]{1,0:T(8,128)(2,1)} %up.1, bf16[896,384]{1,0:T(8,128)(2,1)} %down.1, bf16[16,384]{1,0:T(8,128)(2,1)} %cot.1), custom_call_target="tpu_custom_call" | custom-call | tf_op jit(solution)/shard_map/pallas_call | solution.py:288
  92.7 0.0 copy-start.1
  92.7 1.3 %copy.12 = bf16[16,384]{1,0:T(8,128)(2,1)} copy(bf16[16,384]{1,0:T(8,128)(2,1)} %get-tuple-element.8) | data formatting | bytes 24576
  94.1 0.0 copy-done.1
  94.1 0.6 copy.13
  94.7 0.0 copy-start
  94.7 2.1 %copy.14 = bf16[384,896]{1,0:T(8,128)(2,1)} copy(bf16[384,896]{1,0:T(8,128)(2,1)} %get-tuple-element.10) | data formatting | bytes 1376256
  96.7 0.0 copy-done
  96.7 0.8 copy.15
Async XLA Ops:
  92.7 1.3 %copy-start.1 = (bf16[16,384]{1,0:T(8,128)(2,1)S(1)}, bf16[16,384]{1,0:T(8,128)(2,1)}, u32[]{:S(2)}) copy-start(bf16[16,384]{1,0:T(8,128)(2,1)} %get-tuple-element.9) | copy-start | bytes 36868
  94.7 2.1 %copy-start = (bf16[896,384]{1,0:T(8,128)(2,1)S(1)}, bf16[896,384]{1,0:T(8,128)(2,1)}, u32[]{:S(2)}) copy-start(bf16[896,384]{1,0:T(8,128)(2,1)} %get-tuple-element.11) | copy-start | bytes 2064388

commit v4 on v3

--- a/solution.py
+++ b/solution.py
@@ -20,8 +20,9 @@
 AWAY = (2, 1, -1)
 Z_AWAY = (8,) + tuple(s * k for k in range(7, 0, -1) for s in (1, -1))
 Z_DIRECT = (8, 6, -6, 3, -3, 1, -1)
+FIRST = 7
 N_SEM = 208
-ORDER = "FBFBFFBFBFBFBFFBFBBGBGFB"
+ORDER = "FBFBFFBFBFBFBFFBFBFBBBGGFB"
 GELU_A = math.sqrt(2.0 / math.pi)
 GELU_B = 0.044715
 
@@ -102,7 +103,7 @@
     ]
 
     barrier = pltpu.get_barrier_semaphore()
-    peers = (sibling, partner, *x_devs, *y_devs, *z_devs)
+    peers = (*z_devs, *y_devs, *x_devs, partner, sibling)
     for peer in peers:
         pl.semaphore_signal(barrier, inc=1, device_id=peer, device_id_type=MESH)
     pl.semaphore_wait(barrier, len(peers))
@@ -245,6 +246,8 @@
 
         copies = []
         for i, (k, to) in enumerate(zip(Z_AWAY, z_devs)):
+            if i == FIRST:
+                yield
             across[i].wait_recv()
             zs[a, zrows(k), :] = (total[zrows(k), :] + rb[a, zrows(k), :].astype(F32)).astype(BF16)
             copies.append(send(zs.at[a, zrows(k), :], rz.at[a, i], to))
@@ -326,7 +329,7 @@
             pltpu.SemaphoreType.DMA((8,)),
         ],
         compiler_params=pltpu.CompilerParams(
-            collective_id=0, has_side_effects=True, vmem_limit_bytes=60 * 1024 * 1024
+            collective_id=0, has_side_effects=True, vmem_limit_bytes=52 * 1024 * 1024
         ),
     )(tokens, up_weight, down_weight, out_grad)
 

time: 97.8 us -> 96.7 us (0.989)
  no operation moved by 1% of the time
where the time goes in v4:
time: 96.7 us; the launch traced here: 96.4 us
  Pallas kernels  91.5 us (95%)
  local copies, waits for them, and re-layouts  4.3 us (4%)
    pallas_call x1, Pallas kernels, body(): pl.pallas_call(kernel, out_shape=(jax.ShapeDtypeStruct((ROWS, FEAT), BF16...  91.5 us
    unnamed x8, local copies, waits for them, and re-layouts  4.3 us

profile of v4, /device:TPU:1, one launch (start us, length us, event | category | flops | bytes accessed | tf_op | source)
XLA Modules:
  0.0 96.4 jit_solution(4484707516484765187)
XLA Ops:
  0.6 0.0 copy-start
  0.6 0.7 copy-done
  1.3 0.0 copy-start.1
  1.3 0.7 copy-done.1
  2.0 91.5 %shard_map.75 = (bf16[16,384]{1,0:T(8,128)(2,1)S(1)}, bf16[16,384]{1,0:T(8,128)(2,1)S(1)}, bf16[384,896]{1,0:T(8,128)(2,1)S(1)}, bf16[896,384]{1,0:T(8,128)(2,1)S(1)}) custom-call(bf16[16,384]{1,0:T(8,128)(2,1)S(1)} %copy-done, bf16[384,896]{1,0:T(8,128)(2,1)} %up.1, bf16[896,384]{1,0:T(8,128)(2,1)} %down.1, bf16[16,384]{1,0:T(8,128)(2,1)S(1)} %copy-done.1), custom_call_target="tpu_custom_call" | custom-call | tf_op jit(solution)/shard_map/pallas_call | solution.py:291
  93.5 0.6 copy.12
  94.1 0.6 copy.13
  94.7 0.8 copy.14
  95.6 0.8 copy.15
Async XLA Ops:
  0.6 0.7 copy-start
  1.3 0.7 copy-start.1
